TPU v7x, 256 devices: a whole 4x4x8 slice. The times are simulated.
256 devices in a mesh: seq: 64 (over z_lo, x, y), head: 4 (over z_hi, core).
Axes of the slice: x: 4, y: 4, z: 8 (z_hi: 2, z_lo: 4; z = z_hi * 4 + z_lo), core: 2. Of those that a mesh axis runs over, the one named last changes fastest.
Arguments:
- tokens: bfloat16 [131072, 1024], P('seq'), may hold values from -6 to 6
- norm_gain: float32 [1024], replicated, may hold values from 0.1 to 1.9
- w_qkv: bfloat16 [1024, 3, 1024], P(None, None, 'head'), may hold values from -10.5 to 10.5
- w_out: bfloat16 [1024, 1024], P('head'), may hold values from -0.75 to 0.75
Outputs:
- mixed: float32 [131072, 1024], P(('seq', 'head'))
All inputs are finite; a program needn't handle non-finite values.
Results may differ from a plain program's by a relative error of at most 0.009.
The roundings to bfloat16 on the way count: a program that leaves them out, or rounds other values in their place, can miss the bound.
Values may be sent and summed in bfloat16 or wider, within the bound.
A program may use at most 128 MiB of HBM per device.

v0:
```python
import jax
import jax.numpy as jnp
from jax import lax
from jax.sharding import PartitionSpec as P

HEAD_SIZE = 64
TOK_DEV = 2048
DILATION_MID = 8
DILATION_WHOLE = 64
SEGMENT_MID = 16384


norm_eps = 1e-05


def from_partner(value, axis, bit):
    mask = 2**bit
    pairs = [(source, source ^ mask) for source in range(lax.axis_size(axis))]
    return lax.ppermute(value, axis, pairs)


def layer_norm(token_rows, norm_gain):
    widened = token_rows.astype(jnp.float32)
    center = jnp.mean(widened, axis=-1, keepdims=True)
    variance = jnp.mean((widened - center) ** 2, axis=-1, keepdims=True)
    return ((widened - center) * lax.rsqrt(variance + norm_eps) * norm_gain).astype(jnp.bfloat16)


def attend_heads(query_matrix, keyval):
    half_width = keyval.shape[-1] // 2
    scores = jnp.dot(
        query_matrix, keyval[:, :half_width].T, preferred_element_type=jnp.float32
    ) * half_width ** (-0.5)
    row_peak = jnp.max(scores, axis=-1, keepdims=True)
    expanded = jnp.exp(scores - row_peak)
    row_total = jnp.sum(expanded, axis=-1, keepdims=True)
    probabilities = (expanded / row_total).astype(jnp.bfloat16)
    result = jnp.dot(probabilities, keyval[:, half_width:], preferred_element_type=jnp.float32)
    return (result, row_peak[:, 0] + jnp.log(row_total[:, 0]))


def blend_branches(
    lse_one, out_one, logsumexp_second, output_second, logsumexp_third, output_third
):
    highest = jnp.maximum(jnp.maximum(lse_one, logsumexp_second), logsumexp_third)
    weight_one = jnp.exp(lse_one - highest)[..., None]
    weight_two = jnp.exp(logsumexp_second - highest)[..., None]
    weight_three = jnp.exp(logsumexp_third - highest)[..., None]
    summed = weight_one * out_one + weight_two * output_second + weight_three * output_third
    return summed / (weight_one + weight_two + weight_three)


def pick_rows(blocked, selector):
    stride = selector.shape[0]
    shaped = blocked.reshape((blocked.shape[0] // stride, stride) + blocked.shape[1:])
    chosen = selector.reshape((1,) + selector.shape + (1,) * (blocked.ndim - 2))
    return jnp.sum(jnp.where(chosen, shaped, jnp.zeros((), blocked.dtype)), axis=1)


def spread_back(picked, selector, filler):
    stride = selector.shape[0]
    chosen = selector.reshape((1,) + selector.shape + (1,) * (picked.ndim - 2))
    widened = jnp.where(chosen, jnp.expand_dims(picked, 1), jnp.asarray(filler, picked.dtype))
    return widened.reshape((picked.shape[0] * stride,) + picked.shape[1:])


def on_device(tokens, norm_gain, w_qkv, w_out):
    row_count = tokens.shape[0]
    head_width = w_qkv.shape[2]
    local_heads = head_width // HEAD_SIZE
    normed = layer_norm(tokens, norm_gain)
    projected = jnp.dot(
        normed, w_qkv.reshape(w_qkv.shape[0], 3 * head_width), preferred_element_type=jnp.float32
    ).astype(jnp.bfloat16)
    projected = projected.reshape(row_count, 3, local_heads, HEAD_SIZE)
    query_matrix = projected[:, 0]
    keyval = jnp.concatenate([projected[:, 1], projected[:, 2]], axis=-1)
    head_numbers = lax.axis_index("head") * local_heads + jnp.arange(local_heads, dtype=jnp.int32)
    nearby_selection = (
        jnp.arange(DILATION_MID, dtype=jnp.int32)[:, None] == (head_numbers % DILATION_MID)[None, :]
    )
    distant_selection = (
        jnp.arange(DILATION_WHOLE, dtype=jnp.int32)[:, None]
        == (head_numbers % DILATION_WHOLE)[None, :]
    )
    by_head = jax.vmap(attend_heads, in_axes=(1, 1), out_axes=(1, 1))
    out_one, lse_one = lax.map(
        lambda operands: attend_heads(operands[0], operands[1]),
        (jnp.transpose(query_matrix, (1, 0, 2)), jnp.transpose(keyval, (1, 0, 2))),
    )
    out_one = jnp.transpose(out_one, (1, 0, 2))
    lse_one = lse_one.T
    seq_index = lax.axis_index("seq")
    query_two = pick_rows(query_matrix, nearby_selection)
    group_rows = pick_rows(keyval, nearby_selection)
    group_bits = (SEGMENT_MID // TOK_DEV).bit_length() - 1
    for bit_index in range(group_bits):
        partner = from_partner(group_rows, "seq", bit_index)
        upper_half = seq_index // 2**bit_index % 2 == 1
        group_rows = jnp.where(
            upper_half,
            jnp.concatenate([partner, group_rows], axis=0),
            jnp.concatenate([group_rows, partner], axis=0),
        )
    output_second, logsumexp_second = by_head(query_two, group_rows)
    query_three = pick_rows(query_matrix, distant_selection)
    far_keyval = lax.all_gather(pick_rows(keyval, distant_selection), "seq", axis=0, tiled=True)
    output_third, logsumexp_third = by_head(query_three, far_keyval)
    blended = blend_branches(
        lse_one,
        out_one,
        spread_back(logsumexp_second, nearby_selection, -1e30),
        spread_back(output_second, nearby_selection, 0.0),
        spread_back(logsumexp_third, distant_selection, -1e30),
        spread_back(output_third, distant_selection, 0.0),
    )
    attended = blended.astype(jnp.bfloat16).reshape(row_count, head_width)
    return lax.psum_scatter(
        jnp.dot(attended, w_out, preferred_element_type=jnp.float32).astype(jnp.bfloat16),
        "head",
        scatter_dimension=0,
        tiled=True,
    ).astype(jnp.float32)


def solution(mesh):
    return jax.shard_map(
        on_device,
        mesh=mesh,
        in_specs=(P("seq", None), P(), P(None, None, "head"), P("head", None)),
        out_specs=P(("seq", "head"), None),
        check_vma=False,
    )
```

profile of v0, /device:TPU:40, one launch (start us, length us, event | category | flops | bytes accessed | tf_op | source)
XLA Modules:
  0.0 512.6 jit_solution(8958977734782673796)
XLA Ops:
  6.5 3.0 convert_reduce_fusion
  13.2 6.3 %fusion.29 = bf16[2048,768]{0,1:T(8,128)(2,1)S(1)} fusion(bf16[1024,768]{0,1:T(8,128)(2,1)} %bitcast.123, bf16[2048,1024]{1,0:T(8,128)(2,1)} %param.6, f32[1024]{0:T(1024)S(1)} %copy-done.9, f32[2048]{0:T(1024)S(1)} %add_rsqrt_fusion, f32[2048]{0:T(1024)S(1)} %broadcast_multiply_fusion), kind=kOutput, calls=%fused_computation.42 | convolution fusion | flops 3233284096 | bytes 8933376 | tf_op jit(solution)/shard_map/dot_general | solution.py:72
  23.3 3.3 copy.39
  27.3 3.7 fusion.32
  31.8 7.6 %collective-permute-done = bf16[256,4,128]{0,2,1:T(8,128)(2,1)} collective-permute-done((bf16[256,4,128]{0,2,1:T(8,128)(2,1)S(1)}, bf16[256,4,128]{0,2,1:T(8,128)(2,1)}, u32[]{:S(2)}, u32[]{:S(2)}) %collective-permute-start) | collective-permute-done | bytes 262176 | tf_op jit(solution)/shard_map/ppermute | solution.py:19
  40.6 2.4 collective-permute-start.1
  43.0 3.1 fusion.33
  49.1 4.7 maximum_bitcast_fusion
  55.1 2.5 maximum_select_fusion.3
  59.1 105.3 %while.12 = (s32[]{:T(128)}, f32[4,2048,64]{1,2,0:T(8,128)}, f32[4,2048]{1,0:T(4,128)S(1)}, bf16[4,2048,64]{2,1,0:T(8,128)(2,1)S(1)}, bf16[4,2048,128]{2,1,0:T(8,128)(2,1)}, /*index=5*/s32[]{:T(128)}, s32[]{:T(128)}) while((s32[]{:T(128)}, f32[4,2048,64]{1,2,0:T(8,128)}, f32[4,2048]{1,0:T(4,128)S(1)}, bf16[4,2048,64]{2,1,0:T(8,128)(2,1)S(1)}, ...), condition=%wide.region_5.6_spmd, body=%wide.region_2.5_spmd.sunk | while | flops 1111488512 | bytes 53559896 | solution.py:87
  60.2 8.1 %multiply_reduce_fusion.3 = (f32[2048]{0:T(1024)S(1)}, f32[2048,2048]{0,1:T(8,128)}) fusion(bf16[2048,128]{1,0:T(8,128)(2,1)S(1)} %dynamic-slice_bitcast_fusion.2, bf16[4,2048,64]{2,1,0:T(8,128)(2,1)S(1)} %get-tuple-element.114, s32[]{:T(128)} %get-tuple-element.104), kind=kOutput, calls=%fused_computation.2.clone.1 | convolution fusion | flops 545257472 | bytes 17833988 | tf_op jit(solution)/shard_map/while/body/eval_jaxpr/dot_general | solution.py:31
  68.2 8.6 %fusion.63 = f32[2048]{0:T(1024)S(1)} fusion(f32[2048,2048]{0,1:T(8,128)} %get-tuple-element.95, f32[2048]{0:T(1024)S(1)} %get-tuple-element.96), kind=kLoop, calls=%fused_computation.3.clone.1 | loop fusion | flops 12580864 | bytes 16793600 | tf_op jit(solution)/shard_map/while/body/eval_jaxpr/reduce_sum | solution.py:36
  77.0 8.5 %fusion.64 = f32[4,2048,64]{1,2,0:T(8,128)} fusion(f32[4,2048,64]{1,2,0:T(8,128)} %get-tuple-element.105, s32[]{:T(128)} %get-tuple-element.104, f32[2048,2048]{0,1:T(8,128)} %get-tuple-element.95, f32[2048]{0:T(1024)S(1)} %fusion.63, f32[2048]{0:T(1024)S(1)} %get-tuple-element.96, bf16[2048,128]{1,0:T(8,128)(2,1)S(1)} %dynamic-slice_bitcast_fusion.2), kind=kOutput, calls=%fused_computation.6.clone.1 | convolution fusion | flops 553648128 | bytes 17842688 | tf_op jit(solution)/shard_map/while/body/eval_jaxpr/dot_general | solution.py:38
  86.5 8.1 %multiply_reduce_fusion.3 = (f32[2048]{0:T(1024)S(1)}, f32[2048,2048]{0,1:T(8,128)}) fusion(bf16[2048,128]{1,0:T(8,128)(2,1)S(1)} %dynamic-slice_bitcast_fusion.2, bf16[4,2048,64]{2,1,0:T(8,128)(2,1)S(1)} %get-tuple-element.114, s32[]{:T(128)} %get-tuple-element.104), kind=kOutput, calls=%fused_computation.2.clone.1 | convolution fusion | flops 545257472 | bytes 17833988 | tf_op jit(solution)/shard_map/while/body/eval_jaxpr/dot_general | solution.py:31
  94.6 8.6 %fusion.63 = f32[2048]{0:T(1024)S(1)} fusion(f32[2048,2048]{0,1:T(8,128)} %get-tuple-element.95, f32[2048]{0:T(1024)S(1)} %get-tuple-element.96), kind=kLoop, calls=%fused_computation.3.clone.1 | loop fusion | flops 12580864 | bytes 16793600 | tf_op jit(solution)/shard_map/while/body/eval_jaxpr/reduce_sum | solution.py:36
  103.3 8.5 %fusion.64 = f32[4,2048,64]{1,2,0:T(8,128)} fusion(f32[4,2048,64]{1,2,0:T(8,128)} %get-tuple-element.105, s32[]{:T(128)} %get-tuple-element.104, f32[2048,2048]{0,1:T(8,128)} %get-tuple-element.95, f32[2048]{0:T(1024)S(1)} %fusion.63, f32[2048]{0:T(1024)S(1)} %get-tuple-element.96, bf16[2048,128]{1,0:T(8,128)(2,1)S(1)} %dynamic-slice_bitcast_fusion.2), kind=kOutput, calls=%fused_computation.6.clone.1 | convolution fusion | flops 553648128 | bytes 17842688 | tf_op jit(solution)/shard_map/while/body/eval_jaxpr/dot_general | solution.py:38
  112.8 8.1 %multiply_reduce_fusion.3 = (f32[2048]{0:T(1024)S(1)}, f32[2048,2048]{0,1:T(8,128)}) fusion(bf16[2048,128]{1,0:T(8,128)(2,1)S(1)} %dynamic-slice_bitcast_fusion.2, bf16[4,2048,64]{2,1,0:T(8,128)(2,1)S(1)} %get-tuple-element.114, s32[]{:T(128)} %get-tuple-element.104), kind=kOutput, calls=%fused_computation.2.clone.1 | convolution fusion | flops 545257472 | bytes 17833988 | tf_op jit(solution)/shard_map/while/body/eval_jaxpr/dot_general | solution.py:31
  120.9 8.6 %fusion.63 = f32[2048]{0:T(1024)S(1)} fusion(f32[2048,2048]{0,1:T(8,128)} %get-tuple-element.95, f32[2048]{0:T(1024)S(1)} %get-tuple-element.96), kind=kLoop, calls=%fused_computation.3.clone.1 | loop fusion | flops 12580864 | bytes 16793600 | tf_op jit(solution)/shard_map/while/body/eval_jaxpr/reduce_sum | solution.py:36
  129.6 8.5 %fusion.64 = f32[4,2048,64]{1,2,0:T(8,128)} fusion(f32[4,2048,64]{1,2,0:T(8,128)} %get-tuple-element.105, s32[]{:T(128)} %get-tuple-element.104, f32[2048,2048]{0,1:T(8,128)} %get-tuple-element.95, f32[2048]{0:T(1024)S(1)} %fusion.63, f32[2048]{0:T(1024)S(1)} %get-tuple-element.96, bf16[2048,128]{1,0:T(8,128)(2,1)S(1)} %dynamic-slice_bitcast_fusion.2), kind=kOutput, calls=%fused_computation.6.clone.1 | convolution fusion | flops 553648128 | bytes 17842688 | tf_op jit(solution)/shard_map/while/body/eval_jaxpr/dot_general | solution.py:38
  139.2 8.1 %multiply_reduce_fusion.3 = (f32[2048]{0:T(1024)S(1)}, f32[2048,2048]{0,1:T(8,128)}) fusion(bf16[2048,128]{1,0:T(8,128)(2,1)S(1)} %dynamic-slice_bitcast_fusion.2, bf16[4,2048,64]{2,1,0:T(8,128)(2,1)S(1)} %get-tuple-element.114, s32[]{:T(128)} %get-tuple-element.104), kind=kOutput, calls=%fused_computation.2.clone.1 | convolution fusion | flops 545257472 | bytes 17833988 | tf_op jit(solution)/shard_map/while/body/eval_jaxpr/dot_general | solution.py:31
  147.2 8.6 %fusion.63 = f32[2048]{0:T(1024)S(1)} fusion(f32[2048,2048]{0,1:T(8,128)} %get-tuple-element.95, f32[2048]{0:T(1024)S(1)} %get-tuple-element.96), kind=kLoop, calls=%fused_computation.3.clone.1 | loop fusion | flops 12580864 | bytes 16793600 | tf_op jit(solution)/shard_map/while/body/eval_jaxpr/reduce_sum | solution.py:36
  155.9 8.5 %fusion.64 = f32[4,2048,64]{1,2,0:T(8,128)} fusion(f32[4,2048,64]{1,2,0:T(8,128)} %get-tuple-element.105, s32[]{:T(128)} %get-tuple-element.104, f32[2048,2048]{0,1:T(8,128)} %get-tuple-element.95, f32[2048]{0:T(1024)S(1)} %fusion.63, f32[2048]{0:T(1024)S(1)} %get-tuple-element.96, bf16[2048,128]{1,0:T(8,128)(2,1)S(1)} %dynamic-slice_bitcast_fusion.2), kind=kOutput, calls=%fused_computation.6.clone.1 | convolution fusion | flops 553648128 | bytes 17842688 | tf_op jit(solution)/shard_map/while/body/eval_jaxpr/dot_general | solution.py:38
  164.9 3.8 copy.32
  171.2 3.1 maximum_select_fusion.1
  177.3 2.5 fusion.37
  180.6 181.9 %all-gather.2.cloned.1.call-done = bf16[2048,4,128]{2,1,0:T(4,128)(2,1)} async-done(((bf16[32,4,128]{2,1,0:T(4,128)(2,1)}), bf16[2048,4,128]{2,1,0:T(4,128)(2,1)}) %all-gather.2.cloned.1.call-update) | async-done | bytes 2097168 | tf_op jit(solution)/shard_map/all_gather | solution.py:107
  362.5 5.0 fusion.52
  367.5 2.4 copy.40
  374.8 7.8 %fusion.27 = bf16[2048,4,64]{2,0,1:T(8,128)(2,1)S(1)} fusion(f32[4,2048,64]{2,1,0:T(8,128)S(1)} %copy-done.3, f32[2048,4]{0,1:T(4,128)S(1)} %get-tuple-element.45, f32[32,4,64]{2,0,1:T(8,128)S(1)} %fusion.38, f32[2048,4]{0,1:T(4,128)S(1)} %get-tuple-element.48, f32[256,4,64]{2,0,1:T(8,128)S(1)} %copy.33, f32[2048,4]{0,1:T(4,128)S(1)} %get-tuple-element.46, ...), kind=kLoop, calls=%fused_computation.39 | loop fusion | flops 4718592 | bytes 3588096 | tf_op jit(solution)/shard_map/convert_element_type | solution.py:117
  384.2 4.4 convolution_convert_fusion
  388.6 114.4 %reduce-scatter.2.cloned.1.call-done = bf16[512,1024]{1,0:T(8,128)(2,1)} async-done(((bf16[2048,1024]{1,0:T(8,128)(2,1)}), bf16[512,1024]{1,0:T(8,128)(2,1)}) %reduce-scatter.2.cloned.1.call-update) | async-done | bytes 1048592 | tf_op jit(solution)/shard_map/reduce_scatter | solution.py:118
  503.0 2.8 convert_element_type.42
  (75 shorter events, 33.8 us)
Async XLA Ops:
  6.5 377.6 %copy-start = (bf16[256,1024]{1,0:T(8,128)(2,1)S(1)}, bf16[256,1024]{1,0:T(8,128)(2,1)}, u32[]{:S(2)}) copy-start(bf16[256,1024]{1,0:T(8,128)(2,1)} %param.9) | copy-start | bytes 1572868
  6.5 355.9 %all-gather.2.cloned.1.call-start = ((), (), s32[]{:S(2)}) async-start(), calls=%async_computation.1 | async-start | bytes 2129920 | tf_op jit(solution)/shard_map/all_gather | solution.py:107
  6.5 3.5 copy-start.2
  6.5 4.9 copy-start.4
  9.5 3.7 copy-start.9
  23.3 19.7 %copy-start.1 = (bf16[2048,1,4,64]{3,0,2,1:T(8,128)(2,1)}, bf16[2048,1,4,64]{3,0,2,1:T(8,128)(2,1)S(1)}, u32[]{:S(2)}) copy-start(bf16[2048,1,4,64]{3,0,2,1:T(8,128)(2,1)S(1)} %copy.38) | copy-start | bytes 3145732
  26.7 0.5 copy-start.5
  31.2 8.2 %collective-permute-start = (bf16[256,4,128]{0,2,1:T(8,128)(2,1)S(1)}, bf16[256,4,128]{0,2,1:T(8,128)(2,1)}, u32[]{:S(2)}, u32[]{:S(2)}) collective-permute-start(bf16[256,4,128]{0,2,1:T(8,128)(2,1)S(1)} %copy.26), channel_id=1, source_target_pairs={{0,4},{4,0},{8,12},{12,8},{16,20},{20,16},{24,28},{28,24},{32,36},... | collective-permute-start | bytes 786440 | tf_op jit(solution)/shard_map/ppermute | solution.py:19
  31.8 14.3 %copy-start.7 = (pred[64,4]{0,1:T(4,128)(4,1)}, pred[64,4]{0,1:T(4,128)(4,1)S(1)}, u32[]{:S(2)}) copy-start(pred[64,4]{0,1:T(4,128)(4,1)S(1)} %iota_compare_fusion) | copy-start | bytes 772
  40.6 14.5 %collective-permute-start.1 = (bf16[512,4,128]{0,2,1:T(8,128)(2,1)S(1)}, bf16[512,4,128]{0,2,1:T(8,128)(2,1)}, u32[]{:S(2)}, u32[]{:S(2)}) collective-permute-start(bf16[512,4,128]{0,2,1:T(8,128)(2,1)S(1)} %maximum_select_fusion.4), channel_id=1, source_target_pairs={{0,8},{4,12},{8,0},{12,4},{16,24},{20,28},{24,16},{28,20},{32,40},... | collective-permute-start | bytes 1572872 | tf_op jit(solution)/shard_map/ppermute | solution.py:19
  46.7 456.2 %reduce-scatter.2.cloned.1.call-start = ((), (), s32[]{:S(2)}) async-start(), calls=%async_computation.2 | async-start | bytes 5242880 | tf_op jit(solution)/shard_map/reduce_scatter | solution.py:118
  57.6 113.6 %collective-permute-start.2 = (bf16[1024,4,128]{0,2,1:T(8,128)(2,1)}, bf16[1024,4,128]{0,2,1:T(8,128)(2,1)}, u32[]{:S(2)}, u32[]{:S(2)}) collective-permute-start(bf16[1024,4,128]{0,2,1:T(8,128)(2,1)} %maximum_select_fusion.3), channel_id=1, source_target_pairs={{0,16},{4,20},{8,24},{12,28},{16,0},{20,4},{24,8},{28,12},{32,48},... | collective-permute-start | bytes 3145736 | tf_op jit(solution)/shard_map/ppermute | solution.py:19
  59.1 105.3 %copy-start.6 = (pred[8,4]{0,1:T(4,128)(4,1)S(1)}, pred[8,4]{0,1:T(4,128)(4,1)}, u32[]{:S(2)}) copy-start(pred[8,4]{0,1:T(4,128)(4,1)} %copy-done.5) | copy-start | bytes 100
  59.1 105.7 %copy-start.8 = (pred[64,4]{0,1:T(4,128)(4,1)S(1)}, pred[64,4]{0,1:T(4,128)(4,1)}, u32[]{:S(2)}) copy-start(pred[64,4]{0,1:T(4,128)(4,1)} %copy-done.7) | copy-start | bytes 772
  371.9 2.8 copy-start.3
Sparse Core Ops, SparseCore 0:
  46.9 315.5 all-gather.1
  388.8 114.1 reduce-scatter.1
where the time goes:
time: 516 us; the launch traced here: 513 us
  waiting for transfers between devices  305 us (59%)
  matrix products  84.6 us (16%)
  other arithmetic  72.3 us (14%)
  local copies, waits for them, and re-layouts  32.1 us (6%)
  between operations  13.7 us (3%)
    all_gather x1, waiting for transfers between devices, on_device(): lax.all_gather(pick_rows(keyval, distant_selection), 'seq', axis=0, tiled...  182 us
    reduce_scatter x1, waiting for transfers between devices, on_device(): lax.psum_scatter(jnp.dot(attended, w_out, preferred_element_type=jnp.floa...  114 us
    dot_general x6, matrix products, attend_heads(): jnp.dot(probabilities, keyval[:, half_width:], preferred_element_type=jnp...  38.7 us
    reduce_sum x6, other arithmetic, attend_heads(): row_total = jnp.sum(expanded, axis=-1, keepdims=True)  36.2 us
    dot_general x6, matrix products, attend_heads(): jnp.dot(query_matrix, keyval[:, :half_width].T, preferred_element_type=jn...  35.2 us
    unnamed x25, local copies, waits for them, and re-layouts  13 us
  transfers between devices with their start and end apart: 5, of which 4 were waited for; matrix products, arithmetic and copies ran while one was open for 26% of the time, Pallas kernels for 0%

commit v1 on v0

v1 whole, which is shorter than its diff:
```python
import functools

import jax
import jax.numpy as jnp
from jax import lax
from jax.experimental import pallas as pl
from jax.experimental.pallas import tpu as pltpu
from jax.sharding import PartitionSpec as P

MESH = pl.DeviceIdType.MESH
F32 = jnp.float32
BF16 = jnp.bfloat16
EPS = 1e-05
LOG2E = 1.4426950408889634
HEADS = 4
HEAD = 64
ROWS = 512
FEATS = 256
KEYS = 2048
CHUNK = 256
NEG = -1e30

RELATION = (2, 3, 1, 0)

COPIES = (
    ["wc", "wz", "w2", "mq", "mp"]
    + [f"wy{i}" for i in (1, 2, 3)]
    + [f"wx{i}" for i in (1, 2, 3)]
    + [f"my{i}" for i in (1, 2, 3)]
    + [f"fz{i}" for i in (1, 2, 3)]
    + [f"fy{i}" for i in (1, 2, 3)]
    + [f"fq{i}" for i in (1, 2, 3)]
    + [f"fp{i}" for i in (1, 2, 3)]
    + [f"b{i}" for i in range(3)]
    + [f"f{i}" for i in range(3)]
)
SLOT = {name: i for i, name in enumerate(COPIES)}


def dot(a, b):
    return jnp.dot(a, b, preferred_element_type=F32)


def kernel(
    tokens_hbm, gain_ref, wqkv_hbm, wout_hbm, out_ref,
    tok, wq, normed, pp, kd, qt, vt, kvm, qm, qmp, vtm, kvff, kvf, qff, qf, qfp, vtf,
    pm_own, pm_st, pm_r, pf_st, pf_r, locacc, att_st, att_r, fx_st, fx_r, wo, s0, s1,
    send_sem, recv_sem, tok_sem, w_sem, wo_sem,
):
    seq = lax.axis_index("seq")
    g = lax.axis_index("head")
    zl, x, y = seq // 16, (seq // 4) % 4, seq % 4
    zhi, core = g // 2, g % 2

    def at_y(i):
        return (zl * 16 + x * 4 + (y + i) % 4, g)

    def at_x(i):
        return (zl * 16 + ((x + i) % 4) * 4 + y, g)

    def at_z(i):
        return (((zl + i) % 4) * 16 + x * 4 + y, g)

    x_pair = (zl * 16 + (x + 1 - 2 * (x % 2)) * 4 + y, g)

    def group(k):
        a, b = RELATION[k] // 2, RELATION[k] % 2
        return ((zhi + a) % 2) * 2 + (core + b) % 2

    def at_rel(k):
        return (seq, group(k))

    everyone = [at_y(i) for i in (1, 2, 3)] + [at_x(i) for i in (1, 2, 3)]
    everyone += [at_z(i) for i in (1, 2, 3)] + [at_rel(k) for k in (0, 1, 2)]
    barrier = pltpu.get_barrier_semaphore()
    for device in everyone:
        pl.semaphore_signal(barrier, inc=1, device_id=device, device_id_type=MESH)

    def copy(name):
        piece = pl.ds(pl.multiple_of(16 * (x * 4 + y), 16), 16)
        quarter = pl.ds(pl.multiple_of(64 * x, 64), 64)
        kind, i = name[:-1], name[-1]
        if name == "wc":
            src, dst, dev = wo.at[3], wo.at[2], at_rel(2)
        elif name == "wz":
            src, dst, dev = wo.at[3, piece], wo.at[0, piece], at_rel(0)
        elif name == "w2":
            src, dst, dev = wo.at[0], wo.at[1], at_rel(2)
        elif name == "mq":
            src, dst, dev = qm.at[0], qm.at[1], x_pair
        elif name == "mp":
            src, dst, dev = pm_st, pm_r, x_pair
        elif kind == "wy":
            src, dst, dev = wo.at[0, piece], wo.at[0, piece], at_y(int(i))
        elif kind == "wx":
            src, dst, dev = wo.at[0, quarter], wo.at[0, quarter], at_x(int(i))
        elif kind == "my":
            src, dst, dev = kvm.at[0], kvm.at[int(i)], at_y(int(i))
        elif kind == "fz":
            src, dst, dev = kvf.at[0, 0], kvf.at[0, int(i)], at_z(int(i))
        elif kind == "fy":
            src, dst, dev = kvf.at[0], kvf.at[int(i)], at_y(int(i))
        elif kind == "fq":
            src, dst, dev = qf.at[0], qf.at[int(i)], at_x(int(i))
        elif kind == "fp":
            src, dst, dev = pf_st.at[int(i)], pf_r.at[int(i) - 1], at_x(4 - int(i))
        elif kind == "b":
            src, dst, dev = att_st.at[int(i)], att_r.at[int(i)], at_rel(int(i))
        else:
            src, dst, dev = fx_st.at[int(i)], fx_r.at[int(i)], at_rel(int(i))
        return pltpu.make_async_remote_copy(
            src_ref=src, dst_ref=dst, send_sem=send_sem.at[SLOT[name]], recv_sem=recv_sem.at[SLOT[name]],
            device_id=dev, device_id_type=MESH,
        )

    def start(*names):
        for name in names:
            copy(name).start()

    def arrived(*names):
        for name in names:
            copy(name).wait_recv()

    def three(kind):
        return [f"{kind}{i}" for i in (1, 2, 3)]

    def tok_copy(k):
        rows = pl.ds(pl.multiple_of(group(k) * ROWS, ROWS), ROWS)
        return pltpu.make_async_copy(tokens_hbm.at[rows], tok.at[k], tok_sem.at[k])

    w_copies = [pltpu.make_async_copy(wqkv_hbm.at[i], wq.at[i], w_sem.at[i]) for i in range(3)]
    wo_copy = pltpu.make_async_copy(wout_hbm, wo.at[3], wo_sem)
    tok_copy(0).start()
    for c in w_copies:
        c.start()
    wo_copy.start()
    for k in (1, 2, 3):
        tok_copy(k).start()

    vt[:, HEAD:, :] = jnp.ones((HEADS, 16, KEYS), BF16)
    vtm[:, HEAD:, :] = jnp.ones((HEADS, 16, 1024), BF16)
    vtf[:, HEAD:, :] = jnp.ones((HEADS, 16, 512), BF16)
    qmp[:, HEAD:, :] = jnp.zeros((HEADS, HEAD, 512), BF16)
    qfp[:, HEAD:, :] = jnp.zeros((HEADS, HEAD, 128), BF16)

    odd = pl.multiple_of(256 * core, 256)

    def project(k):
        for part in range(16):
            rows = pl.ds(part * 32, 32)
            wide = tok[k, rows, :].astype(F32)
            center = jnp.mean(wide, axis=1, keepdims=True)
            wide = wide - center
            variance = jnp.mean(wide * wide, axis=1, keepdims=True)
            normed[rows, :] = (wide * lax.rsqrt(variance + EPS) * gain_ref[...]).astype(BF16)
        if k == 0:
            for c in w_copies:
                c.wait()
        for i in range(3):
            for half in range(2):
                result = dot(normed[half * 256:(half + 1) * 256, :], wq[i])
                for m in range(32):
                    b, c = half * 4 + m // 8, m % 8
                    for t in range(2):
                        pp[2 * i + t, pl.ds(8 * c + b, 8, stride=64), :] = result[8 * m:8 * m + 8, 128 * t:128 * t + 128]
        lanes = pl.ds(k * ROWS, ROWS)

        def piece(section, h, rows):
            return pp[2 * section + h // 2, rows, h % 2 * HEAD:h % 2 * HEAD + HEAD]

        for pair in range(2):
            queries = pp[pair].T.astype(BF16).astype(F32) * (0.125 * LOG2E)
            high = queries.astype(BF16)
            low = (queries - high.astype(F32)).astype(BF16)
            values = pp[4 + pair].T.astype(BF16)
            for side in range(2):
                feats = slice(side * HEAD, (side + 1) * HEAD)
                qt[2 * pair + side, :HEAD, lanes] = high[feats]
                qt[2 * pair + side, HEAD:, lanes] = low[feats]
                vt[2 * pair + side, :HEAD, lanes] = values[feats]
        for h in range(HEADS):
            feats = slice(h * HEAD, (h + 1) * HEAD)
            key = piece(1, h, slice(None))
            kd[h, lanes, :] = jnp.concatenate([key, key], axis=1).astype(BF16)
            mid_rows = pl.ds(odd + h * 64, 64)
            far_rows = pl.ds(pl.multiple_of(odd + h * 64 + 8 * zhi, 8), 8)
            pair = jnp.concatenate([piece(1, h, mid_rows), piece(2, h, mid_rows)], axis=1)
            kvm[0, h, k * 64:(k + 1) * 64, :] = pair.astype(BF16)
            qm[0, k * 64:(k + 1) * 64, feats] = piece(0, h, mid_rows).astype(BF16)
            kvff[h, k * 8:(k + 1) * 8, :] = jnp.concatenate([piece(1, h, far_rows), piece(2, h, far_rows)], axis=1)
            qff[k * 8:(k + 1) * 8, feats] = piece(0, h, far_rows)

    for k in range(4):
        tok_copy(k).wait()
        project(k)
        if k == 0:
            pl.semaphore_wait(barrier, len(everyone))
            wo_copy.wait()
            start("wc", "wz")
        if k == 2:
            arrived("wz")
            start(*three("wy"))
    kvf[0, 0] = kvff[...].astype(BF16)
    qf[0] = qff[...].astype(BF16)
    start(*three("fz"), "mq", *three("fq"), *three("my"))

    def top_rows(den8, m):
        row = lax.broadcasted_iota(jnp.int32, den8.shape, 0)
        return jnp.where(row == 0, den8, m)

    def scores(u, slot, c, peak):
        k, h = u // 4, u % 4
        lanes = pl.ds(pl.multiple_of(k * ROWS, ROWS), ROWS)
        s = dot(kd[h, c * CHUNK:(c + 1) * CHUNK, :], qt[h, :, lanes])
        slot[c * CHUNK:(c + 1) * CHUNK, :] = s
        t = jnp.max(s.reshape(CHUNK // 8, 8, ROWS), axis=0)
        return t if peak is None else jnp.maximum(peak, t)

    def weigh(u, slot, c, m, acc):
        h = u % 4
        p = jnp.exp2(slot[c * CHUNK:(c + 1) * CHUNK, :] - m).astype(BF16)
        o = dot(vt[h, :, c * CHUNK:(c + 1) * CHUNK], p)
        return o if acc is None else acc + o

    def finish(u, acc, m):
        k, h = u // 4, u % 4
        feats = pl.ds(pl.multiple_of(h * HEAD, HEAD), HEAD)
        att_st[k, feats, :] = (acc[:HEAD] * (1.0 / acc[HEAD:HEAD + 1])).astype(BF16)
        locacc[k, h, :HEAD, :] = acc[:HEAD]
        locacc[k, h, HEAD:, :] = top_rows(acc[HEAD:HEAD + 8], m)

    def half(u, cur, nxt, m, last=False):
        peak = acc = None
        for c in range(KEYS // CHUNK):
            if not last:
                peak = scores(u + 1, nxt, c, peak)
            acc = weigh(u, cur, c, m, acc)
        finish(u, acc, m)
        return None if last else jnp.max(peak, axis=0, keepdims=True)

    def local(first, final, steps):
        peak = None
        for c in range(KEYS // CHUNK):
            peak = scores(first, s0, c, peak)
        m = jnp.max(peak, axis=0, keepdims=True)

        def body(i, m):
            u = first + 2 * i
            m = half(u, s0, s1, m)
            m = half(u + 1, s1, s0, m)
            for at, step in steps.items():
                pl.when(i == at)(step)
            return m

        m = lax.fori_loop(0, (final - first) // 2 - 1, body, m)
        m = half(final - 2, s0, s1, m)
        half(final - 1, s1, s0, m, last=True)

    def step0():
        arrived(*three("fz"))
        start(*three("fy"))

    def step1():
        start("b0")
        arrived(*three("wy"))
        start(*three("wx"))

    def step3():
        start("b1")
        arrived(*three("wx"))
        start("w2")

    local(0, 12, {0: step0, 1: step1, 3: step3})
    start("b2")

    arrived("mq", *three("my"))
    for i in range(2):
        turned = (qm[i].astype(F32) * 0.125).T.astype(BF16)
        for h in range(HEADS):
            qmp[h, :HEAD, i * 256:(i + 1) * 256] = turned[h * HEAD:(h + 1) * HEAD]
    for i in range(4):
        for h in range(HEADS):
            vtm[h, :HEAD, i * 256:(i + 1) * 256] = kvm[i, h].astype(F32).T[HEAD:].astype(BF16)

    def mid_scores(h, slot, c, peak):
        s = dot(kvm[c, h], qmp[h]) * LOG2E
        slot[c * CHUNK:(c + 1) * CHUNK, :] = s
        t = jnp.max(s.reshape(CHUNK // 8, 8, 512), axis=0)
        return t if peak is None else jnp.maximum(peak, t)

    def mid_weigh(h, slot, c, m, acc):
        p = jnp.exp2(slot[c * CHUNK:(c + 1) * CHUNK, :] - m).astype(BF16)
        o = dot(vtm[h, :, c * CHUNK:(c + 1) * CHUNK], p)
        return o if acc is None else acc + o

    peak = None
    for c in range(4):
        peak = mid_scores(0, s0, c, peak)
    for h in range(HEADS):
        cur, nxt = (s0, s1) if h % 2 == 0 else (s1, s0)
        m = jnp.max(peak, axis=0, keepdims=True)
        peak = acc = None
        for c in range(4):
            if h < 3:
                peak = mid_scores(h + 1, nxt, c, peak)
            acc = mid_weigh(h, cur, c, m, acc)
        tail = top_rows(acc[HEAD:HEAD + 8], m)
        pm_st[h, :HEAD, :] = acc[:HEAD, 256:]
        pm_st[h, HEAD:, :] = tail[:, 256:]
        pm_own[h, :HEAD, :] = acc[:HEAD, :256]
        pm_own[h, HEAD:, :] = tail[:, :256]
    start("mp")

    arrived(*three("fy"), *three("fq"))
    gathered = jnp.concatenate([qf[i] for i in range(4)], axis=0)
    turned = (gathered.astype(F32) * 0.125).T.astype(BF16)
    far_parts = []
    for h in range(HEADS):
        qfp[h, :HEAD, :] = turned[h * HEAD:(h + 1) * HEAD]
        keyval = kvf[:, :, h].reshape(512, 128)
        vtf[h, :HEAD, :] = keyval.astype(F32).T[HEAD:].astype(BF16)
        s = dot(keyval, qfp[h]) * LOG2E
        m = jnp.max(s, axis=0, keepdims=True)
        p = jnp.exp2(s - m).astype(BF16)
        acc = dot(vtf[h], p)
        far_parts.append(jnp.concatenate([acc[:HEAD], top_rows(acc[HEAD:HEAD + 8], m)], axis=0))
    lane = lax.broadcasted_iota(jnp.int32, (72, 128), 1)
    for i in range(4):
        packed = None
        for h in range(HEADS):
            shift = (32 * h - 32 * i) % 128
            moved = far_parts[h] if shift == 0 else pltpu.roll(far_parts[h], shift, 1)
            packed = moved if packed is None else jnp.where(lane // 32 == h, moved, packed)
        pf_st[i] = packed
    start(*three("fp"))

    local(12, 16, {})

    arrived(*three("fp"))
    parts = [pf_st[0]] + [pf_r[i] for i in range(3)]
    far_m = parts[0][65:66]
    for part in parts[1:]:
        far_m = jnp.maximum(far_m, part[65:66])
    far = None
    for part in parts:
        scaled = part[:72] * jnp.exp2(part[65:66] - far_m)
        far = scaled if far is None else far + scaled
    row = lax.broadcasted_iota(jnp.int32, (72, 128), 0)
    far = jnp.where(row >= 65, far_m, far)
    src = lax.broadcasted_iota(jnp.int32, (128, 256), 0)
    dst = lax.broadcasted_iota(jnp.int32, (128, 256), 1)
    place = (src % 32) // 8 * 64 + 8 * zhi + src % 8 == dst
    active = (lax.broadcasted_iota(jnp.int32, (1, 256), 1) % 64) // 8 == zhi

    arrived("mp")
    half_lane = lax.broadcasted_iota(jnp.int32, (HEAD, 128), 1) < 64
    fixes = {}
    for h in range(HEADS):
        spread = jnp.dot(
            far, jnp.where(place & (src // 32 == h), 1.0, 0.0), precision=lax.Precision.HIGHEST, preferred_element_type=F32
        )
        n_f, d_f = spread[:HEAD], spread[HEAD:HEAD + 1]
        m_f = jnp.where(active, spread[65:66], NEG)
        n_a, d_a, m_a = pm_own[h, :HEAD], pm_own[h, HEAD:HEAD + 1], pm_own[h, HEAD + 1:HEAD + 2]
        n_b, d_b, m_b = pm_r[h, :HEAD], pm_r[h, HEAD:HEAD + 1], pm_r[h, HEAD + 1:HEAD + 2]
        top = jnp.maximum(jnp.maximum(m_a, m_b), m_f)
        w_a, w_b, w_f = jnp.exp2(m_a - top), jnp.exp2(m_b - top), jnp.exp2(m_f - top)
        num = w_a * n_a + w_b * n_b + w_f * n_f
        den = w_a * d_a + w_b * d_b + w_f * d_f
        for k in range(4):
            lanes = slice(k // 2 * 128, k // 2 * 128 + 128)
            n_m, d_m, m_m = num[:, lanes], den[:, lanes], top[:, lanes]
            if k % 2 != h % 2:
                n_m, d_m, m_m = (pltpu.roll(v, 64, 1) for v in (n_m, d_m, m_m))
            here = pl.ds(odd + 128 * (h // 2), 128)
            n_l = locacc[k, h, :HEAD, here]
            tail = locacc[k, h, HEAD:, here]
            d_l, m_l = tail[0:1], tail[1:2]
            peak = jnp.maximum(m_l, m_m)
            w_l, w_m = jnp.exp2(m_l - peak), jnp.exp2(m_m - peak)
            fixes[k, h] = (w_l * n_l + w_m * n_m) / (w_l * d_l + w_m * d_m)
    for k in range(4):
        for pair in range(2):
            both = jnp.where(half_lane, fixes[k, 2 * pair], fixes[k, 2 * pair + 1])
            fx_st[k, pair * HEAD:(pair + 1) * HEAD, :] = both.astype(BF16)
        if k < 3:
            start(f"f{k}")

    def contribution(k):
        att, fix = (att_st, fx_st) if k == 3 else (att_r, fx_r)
        side = pl.multiple_of(256 * ((core + RELATION[k]) % 2), 256)
        for h in range(HEADS):
            feats, here = pl.ds(h * HEAD, HEAD), pl.ds(side + 128 * (h // 2), 128)
            new = fix[k, h // 2 * HEAD:(h // 2 + 1) * HEAD, :]
            mine = half_lane if h % 2 == 0 else jnp.logical_not(half_lane)
            att[k, feats, here] = jnp.where(mine, new, att[k, feats, here])
        turned = att[k].astype(F32).T
        for m in range(64):
            for t in range(2):
                pp[t, pl.ds(8 * (m % 8) + m // 8, 8, stride=64), :] = turned[8 * m:8 * m + 8, 128 * t:128 * t + 128]
        rows = jnp.concatenate([pp[0], pp[1]], axis=1).astype(BF16)
        return dot(rows, wo[k]).astype(BF16).astype(F32)

    for n, k in enumerate((3, 2, 0, 1)):
        if k < 3:
            arrived(f"b{k}", f"f{k}")
        if k == 1:
            arrived("w2")
        if k == 2:
            arrived("wc")
        if n == 0:
            out_ref[...] = contribution(k)
        else:
            out_ref[...] += contribution(k)
    for name in COPIES:
        copy(name).wait_send()


def on_device(tokens, norm_gain, w_qkv, w_out):
    vm = pltpu.VMEM
    return pl.pallas_call(
        kernel,
        out_shape=jax.ShapeDtypeStruct((ROWS, 1024), F32),
        in_specs=[
            pl.BlockSpec(memory_space=pl.ANY),
            pl.BlockSpec(memory_space=pltpu.VMEM),
            pl.BlockSpec(memory_space=pl.ANY),
            pl.BlockSpec(memory_space=pl.ANY),
        ],
        out_specs=pl.BlockSpec(memory_space=pltpu.VMEM),
        scratch_shapes=[
            vm((4, ROWS, 1024), BF16),
            vm((3, 1024, FEATS), BF16),
            vm((ROWS, 1024), BF16),
            vm((6, ROWS, 128), F32),
            vm((HEADS, KEYS, 128), BF16),
            vm((HEADS, 128, KEYS), BF16),
            vm((HEADS, 80, KEYS), BF16),
            vm((4, HEADS, 256, 128), BF16),
            vm((2, 256, FEATS), BF16),
            vm((HEADS, 128, 512), BF16),
            vm((HEADS, 80, 1024), BF16),
            vm((HEADS, 32, 128), F32),
            vm((4, 4, HEADS, 32, 128), BF16),
            vm((32, FEATS), F32),
            vm((4, 32, FEATS), BF16),
            vm((HEADS, 128, 128), BF16),
            vm((HEADS, 80, 512), BF16),
            vm((HEADS, 72, 256), F32),
            vm((HEADS, 72, 256), F32),
            vm((HEADS, 72, 256), F32),
            vm((4, 72, 128), F32),
            vm((3, 72, 128), F32),
            vm((4, HEADS, 72, ROWS), F32),
            vm((4, FEATS, ROWS), BF16),
            vm((3, FEATS, ROWS), BF16),
            vm((4, 128, 128), BF16),
            vm((3, 128, 128), BF16),
            vm((4, FEATS, 1024), BF16),
            vm((KEYS, ROWS), F32),
            vm((KEYS, ROWS), F32),
            pltpu.SemaphoreType.DMA((len(COPIES),)),
            pltpu.SemaphoreType.DMA((len(COPIES),)),
            pltpu.SemaphoreType.DMA((4,)),
            pltpu.SemaphoreType.DMA((3,)),
            pltpu.SemaphoreType.DMA,
        ],
        compiler_params=pltpu.CompilerParams(
            collective_id=0, has_side_effects=True, vmem_limit_bytes=56 * 1024 * 1024
        ),
    )(tokens, norm_gain.reshape(1, 1024), jnp.transpose(w_qkv, (1, 0, 2)), w_out)


def solution(mesh):
    return jax.shard_map(
        on_device,
        mesh=mesh,
        in_specs=(P("seq", None), P(), P(None, None, "head"), P("head", None)),
        out_specs=P(("seq", "head"), None),
        check_vma=False,
    )
```

time: 516 us -> 60.3 us (0.12)
  waiting for transfers between devices: 305 us -> 0 us
  matrix products: 84.6 us -> 0 us
  other arithmetic: 72.3 us -> 0 us
  Pallas kernels: 0 us -> 56.7 us
  local copies, waits for them, and re-layouts: 32.1 us -> 3.16 us
  between operations: 13.7 us -> 0.01 us
    all_gather x1 -> x0, waiting for transfers between devices: 182 us -> none  [on_device(): lax.all_gather(pick_rows(keyval, distant_selection), 'seq', axis=0, tiled...]
    reduce_scatter x1 -> x0, waiting for transfers between devices: 114 us -> none  [on_device(): lax.psum_scatter(jnp.dot(attended, w_out, preferred_element_type=jnp.floa...]
    dot_general x14 -> x0, matrix products: 84.6 us -> none  [the longest x6 38.7 us: attend_heads(): jnp.dot(probabilities, keyval[:, half_width:], preferred_element_type=jnp...]
    pallas_call x0 -> x1, Pallas kernels: none -> 56.7 us  [on_device(): pl.pallas_call(kernel, out_shape=jax.ShapeDtypeStruct((ROWS, 1024), F32),...]
    reduce_sum x12 -> x0, other arithmetic: 49.9 us -> none  [the longest x6 36.2 us: attend_heads(): row_total = jnp.sum(expanded, axis=-1, keepdims=True)]
    convert_element_type x2 -> x0, other arithmetic: 10.6 us -> none  [the longest x1 7.79 us: on_device(): attended = blended.astype(jnp.bfloat16).reshape(row_count, head_width)]
    unnamed x25 -> x1, local copies, waits for them, and re-layouts: 13 us -> 3.16 us
    ppermute x3 -> x0, waiting for transfers between devices: 9.01 us -> none  [from_partner(): return lax.ppermute(value, axis, pairs)]
  transfers between devices with their start and end apart: 5 -> 0, of which waited for: 4 -> 0; matrix products, arithmetic and copies ran while one was open for 26% -> 0% of each run, Pallas kernels for 0% -> 0%
where the time goes in v1:
time: 60.3 us; the launch traced here: 59.9 us
  Pallas kernels  56.7 us (94%)
  local copies, waits for them, and re-layouts  3.16 us (5%)
    pallas_call x1, Pallas kernels, on_device(): pl.pallas_call(kernel, out_shape=jax.ShapeDtypeStruct((ROWS, 1024), F32),...  56.7 us
    unnamed x1, local copies, waits for them, and re-layouts  3.16 us

profile of v1, /device:TPU:40, one launch (start us, length us, event | category | flops | bytes accessed | tf_op | source)
XLA Modules:
  0.0 59.9 jit_solution(9480593685680875275)
XLA Ops:
  0.0 56.7 %shard_map.46 = f32[512,1024]{1,0:T(8,128)} custom-call(bf16[2048,1024]{1,0:T(8,128)(2,1)} %tokens_hbm.1, f32[1,1024]{1,0:T(1,128)} %bitcast.3, bf16[3,1024,256]{2,1,0:T(8,128)(2,1)} %bitcast.2, bf16[256,1024]{1,0:T(8,128)(2,1)} %wout_hbm.1), custom_call_target="tpu_custom_call" | custom-call | tf_op jit(solution)/shard_map/pallas_call | solution.py:421
  56.7 3.2 %copy.6 = f32[512,1024]{1,0:T(8,128)} copy(f32[512,1024]{1,0:T(8,128)} %shard_map.46) | data formatting | bytes 4194304

commit v2 on v1

--- a/solution.py
+++ b/solution.py
@@ -26,12 +26,12 @@
     ["wc", "wz", "w2", "mq", "mp"]
     + [f"wy{i}" for i in (1, 2, 3)]
     + [f"wx{i}" for i in (1, 2, 3)]
-    + [f"my{i}" for i in (1, 2, 3)]
+    + [f"m{k}{i}" for k in range(4) for i in (1, 2, 3)]
     + [f"fz{i}" for i in (1, 2, 3)]
     + [f"fy{i}" for i in (1, 2, 3)]
     + [f"fq{i}" for i in (1, 2, 3)]
     + [f"fp{i}" for i in (1, 2, 3)]
-    + [f"b{i}" for i in range(3)]
+    + [f"b{u}" for u in range(12)]
     + [f"f{i}" for i in range(3)]
 )
 SLOT = {name: i for i, name in enumerate(COPIES)}
@@ -44,7 +44,7 @@
 def kernel(
     tokens_hbm, gain_ref, wqkv_hbm, wout_hbm, out_ref,
     tok, wq, normed, pp, kd, qt, vt, kvm, qm, qmp, vtm, kvff, kvf, qff, qf, qfp, vtf,
-    pm_own, pm_st, pm_r, pf_st, pf_r, locacc, att_st, att_r, fx_st, fx_r, wo, s0, s1,
+    pm_own, pm_st, pm_r, pf_st, pf_r, locacc, att_st, att_r, fx_st, fx_r, wo, s0, s1, s2, mid_all,
     send_sem, recv_sem, tok_sem, w_sem, wo_sem,
 ):
     seq = lax.axis_index("seq")
@@ -75,6 +75,15 @@
     barrier = pltpu.get_barrier_semaphore()
     for device in everyone:
         pl.semaphore_signal(barrier, inc=1, device_id=device, device_id_type=MESH)
+
+    def unit_copy(u):
+        k, feats = u // 4, pl.ds(pl.multiple_of(u % 4 * HEAD, HEAD), HEAD)
+        there = ((zhi + 1 - k // 2) % 2) * 2 + (core + (k + 1) // 2) % 2
+        return pltpu.make_async_remote_copy(
+            src_ref=att_st.at[k, feats], dst_ref=att_r.at[k, feats],
+            send_sem=send_sem.at[SLOT["b0"] + u], recv_sem=recv_sem.at[SLOT["b0"] + u],
+            device_id=(seq, there), device_id_type=MESH,
+        )
 
     def copy(name):
         piece = pl.ds(pl.multiple_of(16 * (x * 4 + y), 16), 16)
@@ -94,8 +103,8 @@
             src, dst, dev = wo.at[0, piece], wo.at[0, piece], at_y(int(i))
         elif kind == "wx":
             src, dst, dev = wo.at[0, quarter], wo.at[0, quarter], at_x(int(i))
-        elif kind == "my":
-            src, dst, dev = kvm.at[0], kvm.at[int(i)], at_y(int(i))
+        elif kind[0] == "m":
+            src, dst, dev = kvm.at[0, int(kind[1])], kvm.at[int(i), int(kind[1])], at_y(int(i))
         elif kind == "fz":
             src, dst, dev = kvf.at[0, 0], kvf.at[0, int(i)], at_z(int(i))
         elif kind == "fy":
@@ -104,8 +113,8 @@
             src, dst, dev = qf.at[0], qf.at[int(i)], at_x(int(i))
         elif kind == "fp":
             src, dst, dev = pf_st.at[int(i)], pf_r.at[int(i) - 1], at_x(4 - int(i))
-        elif kind == "b":
-            src, dst, dev = att_st.at[int(i)], att_r.at[int(i)], at_rel(int(i))
+        elif name[0] == "b":
+            return unit_copy(int(name[1:]))
         else:
             src, dst, dev = fx_st.at[int(i)], fx_r.at[int(i)], at_rel(int(i))
         return pltpu.make_async_remote_copy(
@@ -145,64 +154,84 @@
 
     odd = pl.multiple_of(256 * core, 256)
 
-    def project(k):
-        for part in range(16):
-            rows = pl.ds(part * 32, 32)
-            wide = tok[k, rows, :].astype(F32)
-            center = jnp.mean(wide, axis=1, keepdims=True)
-            wide = wide - center
-            variance = jnp.mean(wide * wide, axis=1, keepdims=True)
-            normed[rows, :] = (wide * lax.rsqrt(variance + EPS) * gain_ref[...]).astype(BF16)
-        if k == 0:
-            for c in w_copies:
-                c.wait()
-        for i in range(3):
-            for half in range(2):
-                result = dot(normed[half * 256:(half + 1) * 256, :], wq[i])
-                for m in range(32):
-                    b, c = half * 4 + m // 8, m % 8
-                    for t in range(2):
-                        pp[2 * i + t, pl.ds(8 * c + b, 8, stride=64), :] = result[8 * m:8 * m + 8, 128 * t:128 * t + 128]
+    def norm_part(k, part):
+        rows = pl.ds(part * 32, 32)
+        wide = tok[k, rows, :].astype(F32)
+        center = jnp.mean(wide, axis=1, keepdims=True)
+        wide = wide - center
+        variance = jnp.mean(wide * wide, axis=1, keepdims=True)
+        normed[k % 2, rows, :] = (wide * lax.rsqrt(variance + EPS) * gain_ref[...]).astype(BF16)
+
+    def project_part(k, i, half):
+        result = dot(normed[k % 2, half * 256:(half + 1) * 256, :], wq[i])
+        for m in range(32):
+            b, c = half * 4 + m // 8, m % 8
+            for t in range(2):
+                pp[k % 2, 2 * i + t, pl.ds(8 * c + b, 8, stride=64), :] = result[8 * m:8 * m + 8, 128 * t:128 * t + 128]
+
+    def piece(k, section, h, rows):
+        return pp[k % 2, 2 * section + h // 2, rows, h % 2 * HEAD:h % 2 * HEAD + HEAD]
+
+    def pick_part(k, h):
+        feats = slice(h * HEAD, (h + 1) * HEAD)
+        mid_rows = pl.ds(odd + h * 64, 64)
+        far_rows = pl.ds(pl.multiple_of(odd + h * 64 + 8 * zhi, 8), 8)
+        pair = jnp.concatenate([piece(k, 1, h, mid_rows), piece(k, 2, h, mid_rows)], axis=1)
+        kvm[0, k, h] = pair.astype(BF16)
+        qm[0, k * 64:(k + 1) * 64, feats] = piece(k, 0, h, mid_rows).astype(BF16)
+        kvff[h, k * 8:(k + 1) * 8, :] = jnp.concatenate([piece(k, 1, h, far_rows), piece(k, 2, h, far_rows)], axis=1)
+        qff[k * 8:(k + 1) * 8, feats] = piece(k, 0, h, far_rows)
+
+    def key_part(k, h):
+        key = piece(k, 1, h, slice(None))
+        kd[h, pl.ds(k * ROWS, ROWS), :] = jnp.concatenate([key, key], axis=1).astype(BF16)
+
+    def turn_part(k, pair):
         lanes = pl.ds(k * ROWS, ROWS)
-
-        def piece(section, h, rows):
-            return pp[2 * section + h // 2, rows, h % 2 * HEAD:h % 2 * HEAD + HEAD]
-
-        for pair in range(2):
-            queries = pp[pair].T.astype(BF16).astype(F32) * (0.125 * LOG2E)
-            high = queries.astype(BF16)
-            low = (queries - high.astype(F32)).astype(BF16)
-            values = pp[4 + pair].T.astype(BF16)
-            for side in range(2):
-                feats = slice(side * HEAD, (side + 1) * HEAD)
-                qt[2 * pair + side, :HEAD, lanes] = high[feats]
-                qt[2 * pair + side, HEAD:, lanes] = low[feats]
-                vt[2 * pair + side, :HEAD, lanes] = values[feats]
-        for h in range(HEADS):
-            feats = slice(h * HEAD, (h + 1) * HEAD)
-            key = piece(1, h, slice(None))
-            kd[h, lanes, :] = jnp.concatenate([key, key], axis=1).astype(BF16)
-            mid_rows = pl.ds(odd + h * 64, 64)
-            far_rows = pl.ds(pl.multiple_of(odd + h * 64 + 8 * zhi, 8), 8)
-            pair = jnp.concatenate([piece(1, h, mid_rows), piece(2, h, mid_rows)], axis=1)
-            kvm[0, h, k * 64:(k + 1) * 64, :] = pair.astype(BF16)
-            qm[0, k * 64:(k + 1) * 64, feats] = piece(0, h, mid_rows).astype(BF16)
-            kvff[h, k * 8:(k + 1) * 8, :] = jnp.concatenate([piece(1, h, far_rows), piece(2, h, far_rows)], axis=1)
-            qff[k * 8:(k + 1) * 8, feats] = piece(0, h, far_rows)
-
-    for k in range(4):
-        tok_copy(k).wait()
-        project(k)
+        queries = pp[k % 2, pair].T.astype(BF16).astype(F32) * (0.125 * LOG2E)
+        high = queries.astype(BF16)
+        low = (queries - high.astype(F32)).astype(BF16)
+        values = pp[k % 2, 4 + pair].T.astype(BF16)
+        for side in range(2):
+            feats = slice(side * HEAD, (side + 1) * HEAD)
+            qt[2 * pair + side, :HEAD, lanes] = high[feats]
+            qt[2 * pair + side, HEAD:, lanes] = low[feats]
+            vt[2 * pair + side, :HEAD, lanes] = values[feats]
+
+    tok_copy(0).wait()
+    for part in range(16):
+        norm_part(0, part)
+    for c in w_copies:
+        c.wait()
+    for k in range(5):
+        mxu = [functools.partial(project_part, k, i, side) for i in (1, 2, 0) for side in range(2)] if k < 4 else []
+        beside = []
+        if k > 0:
+            beside += [functools.partial(pick_part, k - 1, h) for h in range(HEADS)]
+        if k < 3:
+            tok_copy(k + 1).wait()
+            beside += [functools.partial(norm_part, k + 1, part) for part in range(16)]
+        if k > 0:
+            beside += [functools.partial(key_part, k - 1, h) for h in range(HEADS)]
+            beside += [functools.partial(turn_part, k - 1, pair) for pair in range(2)]
+        for n in range(max(len(mxu), 1)):
+            if mxu:
+                mxu[n]()
+            share = len(beside) / max(len(mxu), 1)
+            for item in beside[round(n * share):round((n + 1) * share)]:
+                item()
         if k == 0:
             pl.semaphore_wait(barrier, len(everyone))
             wo_copy.wait()
             start("wc", "wz")
-        if k == 2:
+        else:
+            start(*three(f"m{k - 1}"))
+        if k == 3:
             arrived("wz")
             start(*three("wy"))
     kvf[0, 0] = kvff[...].astype(BF16)
     qf[0] = qff[...].astype(BF16)
-    start(*three("fz"), "mq", *three("fq"), *three("my"))
+    start(*three("fz"), "mq", *three("fq"))
 
     def top_rows(den8, m):
         row = lax.broadcasted_iota(jnp.int32, den8.shape, 0)
@@ -238,52 +267,37 @@
         finish(u, acc, m)
         return None if last else jnp.max(peak, axis=0, keepdims=True)
 
-    def local(first, final, steps):
-        peak = None
-        for c in range(KEYS // CHUNK):
-            peak = scores(first, s0, c, peak)
-        m = jnp.max(peak, axis=0, keepdims=True)
-
+    def local(first, m):
         def body(i, m):
             u = first + 2 * i
             m = half(u, s0, s1, m)
+            if first < 12:
+                unit_copy(u).start()
             m = half(u + 1, s1, s0, m)
-            for at, step in steps.items():
-                pl.when(i == at)(step)
+            if first < 12:
+                unit_copy(u + 1).start()
             return m
 
-        m = lax.fori_loop(0, (final - first) // 2 - 1, body, m)
-        m = half(final - 2, s0, s1, m)
-        half(final - 1, s1, s0, m, last=True)
-
-    def step0():
-        arrived(*three("fz"))
-        start(*three("fy"))
-
-    def step1():
-        start("b0")
-        arrived(*three("wy"))
-        start(*three("wx"))
-
-    def step3():
-        start("b1")
-        arrived(*three("wx"))
-        start("w2")
-
-    local(0, 12, {0: step0, 1: step1, 3: step3})
-    start("b2")
-
-    arrived("mq", *three("my"))
+        return lax.fori_loop(0, 2, body, m)
+
+    peak = None
+    for c in range(KEYS // CHUNK):
+        peak = scores(0, s0, c, peak)
+    local_m = local(0, jnp.max(peak, axis=0, keepdims=True))
+    arrived(*three("fz"), *three("wy"))
+    start(*three("fy"), *three("wx"))
+
+    arrived("mq", *[name for k in range(4) for name in three(f"m{k}")])
     for i in range(2):
         turned = (qm[i].astype(F32) * 0.125).T.astype(BF16)
         for h in range(HEADS):
             qmp[h, :HEAD, i * 256:(i + 1) * 256] = turned[h * HEAD:(h + 1) * HEAD]
     for i in range(4):
         for h in range(HEADS):
-            vtm[h, :HEAD, i * 256:(i + 1) * 256] = kvm[i, h].astype(F32).T[HEAD:].astype(BF16)
+            vtm[h, :HEAD, i * 256:(i + 1) * 256] = kvm[i, :, h].reshape(256, 128).astype(F32).T[HEAD:].astype(BF16)
 
     def mid_scores(h, slot, c, peak):
-        s = dot(kvm[c, h], qmp[h]) * LOG2E
+        s = dot(kvm[c, :, h].reshape(256, 128), qmp[h]) * LOG2E
         slot[c * CHUNK:(c + 1) * CHUNK, :] = s
         t = jnp.max(s.reshape(CHUNK // 8, 8, 512), axis=0)
         return t if peak is None else jnp.maximum(peak, t)
@@ -295,9 +309,9 @@
 
     peak = None
     for c in range(4):
-        peak = mid_scores(0, s0, c, peak)
+        peak = mid_scores(0, s1, c, peak)
     for h in range(HEADS):
-        cur, nxt = (s0, s1) if h % 2 == 0 else (s1, s0)
+        cur, nxt = (s1, s2) if h % 2 == 0 else (s2, s1)
         m = jnp.max(peak, axis=0, keepdims=True)
         peak = acc = None
         for c in range(4):
@@ -310,6 +324,10 @@
         pm_own[h, :HEAD, :] = acc[:HEAD, :256]
         pm_own[h, HEAD:, :] = tail[:, :256]
     start("mp")
+
+    local_m = local(4, local_m)
+    arrived(*three("wx"))
+    start("w2")
 
     arrived(*three("fy"), *three("fq"))
     gathered = jnp.concatenate([qf[i] for i in range(4)], axis=0)
@@ -334,7 +352,7 @@
         pf_st[i] = packed
     start(*three("fp"))
 
-    local(12, 16, {})
+    local_m = local(8, local_m)
 
     arrived(*three("fp"))
     parts = [pf_st[0]] + [pf_r[i] for i in range(3)]
@@ -354,7 +372,6 @@
 
     arrived("mp")
     half_lane = lax.broadcasted_iota(jnp.int32, (HEAD, 128), 1) < 64
-    fixes = {}
     for h in range(HEADS):
         spread = jnp.dot(
             far, jnp.where(place & (src // 32 == h), 1.0, 0.0), precision=lax.Precision.HIGHEST, preferred_element_type=F32
@@ -367,24 +384,37 @@
         w_a, w_b, w_f = jnp.exp2(m_a - top), jnp.exp2(m_b - top), jnp.exp2(m_f - top)
         num = w_a * n_a + w_b * n_b + w_f * n_f
         den = w_a * d_a + w_b * d_b + w_f * d_f
-        for k in range(4):
-            lanes = slice(k // 2 * 128, k // 2 * 128 + 128)
-            n_m, d_m, m_m = num[:, lanes], den[:, lanes], top[:, lanes]
+        mid_all[h, :HEAD, :] = num
+        mid_all[h, HEAD:, :] = top_rows(jnp.broadcast_to(den, (8, 256)), top)
+
+    def fix_block(k):
+        lanes = slice(k // 2 * 128, k // 2 * 128 + 128)
+        fixed = []
+        for h in range(HEADS):
+            n_m, tail = mid_all[h, :HEAD, lanes], mid_all[h, HEAD:, lanes]
             if k % 2 != h % 2:
-                n_m, d_m, m_m = (pltpu.roll(v, 64, 1) for v in (n_m, d_m, m_m))
+                n_m, tail = pltpu.roll(n_m, 64, 1), pltpu.roll(tail, 64, 1)
+            d_m, m_m = tail[0:1], tail[1:2]
             here = pl.ds(odd + 128 * (h // 2), 128)
             n_l = locacc[k, h, :HEAD, here]
             tail = locacc[k, h, HEAD:, here]
             d_l, m_l = tail[0:1], tail[1:2]
             peak = jnp.maximum(m_l, m_m)
             w_l, w_m = jnp.exp2(m_l - peak), jnp.exp2(m_m - peak)
-            fixes[k, h] = (w_l * n_l + w_m * n_m) / (w_l * d_l + w_m * d_m)
-    for k in range(4):
+            fixed.append((w_l * n_l + w_m * n_m) / (w_l * d_l + w_m * d_m))
         for pair in range(2):
-            both = jnp.where(half_lane, fixes[k, 2 * pair], fixes[k, 2 * pair + 1])
+            both = jnp.where(half_lane, fixed[2 * pair], fixed[2 * pair + 1])
             fx_st[k, pair * HEAD:(pair + 1) * HEAD, :] = both.astype(BF16)
-        if k < 3:
-            start(f"f{k}")
+
+    for k in range(3):
+        fix_block(k)
+        start(f"f{k}")
+
+    local_m = half(12, s0, s1, local_m)
+    local_m = half(13, s1, s0, local_m)
+    local_m = half(14, s0, s1, local_m)
+    half(15, s1, s0, local_m, last=True)
+    fix_block(3)
 
     def contribution(k):
         att, fix = (att_st, fx_st) if k == 3 else (att_r, fx_r)
@@ -397,13 +427,13 @@
         turned = att[k].astype(F32).T
         for m in range(64):
             for t in range(2):
-                pp[t, pl.ds(8 * (m % 8) + m // 8, 8, stride=64), :] = turned[8 * m:8 * m + 8, 128 * t:128 * t + 128]
-        rows = jnp.concatenate([pp[0], pp[1]], axis=1).astype(BF16)
+                pp[0, t, pl.ds(8 * (m % 8) + m // 8, 8, stride=64), :] = turned[8 * m:8 * m + 8, 128 * t:128 * t + 128]
+        rows = jnp.concatenate([pp[0, 0], pp[0, 1]], axis=1).astype(BF16)
         return dot(rows, wo[k]).astype(BF16).astype(F32)
 
     for n, k in enumerate((3, 2, 0, 1)):
         if k < 3:
-            arrived(f"b{k}", f"f{k}")
+            arrived(*[f"b{4 * k + h}" for h in range(HEADS)], f"f{k}")
         if k == 1:
             arrived("w2")
         if k == 2:
@@ -431,12 +461,12 @@
         scratch_shapes=[
             vm((4, ROWS, 1024), BF16),
             vm((3, 1024, FEATS), BF16),
-            vm((ROWS, 1024), BF16),
-            vm((6, ROWS, 128), F32),
+            vm((2, ROWS, 1024), BF16),
+            vm((2, 6, ROWS, 128), F32),
             vm((HEADS, KEYS, 128), BF16),
             vm((HEADS, 128, KEYS), BF16),
             vm((HEADS, 80, KEYS), BF16),
-            vm((4, HEADS, 256, 128), BF16),
+            vm((4, 4, HEADS, 64, 128), BF16),
             vm((2, 256, FEATS), BF16),
             vm((HEADS, 128, 512), BF16),
             vm((HEADS, 80, 1024), BF16),
@@ -459,6 +489,8 @@
             vm((4, FEATS, 1024), BF16),
             vm((KEYS, ROWS), F32),
             vm((KEYS, ROWS), F32),
+            vm((1024, ROWS), F32),
+            vm((HEADS, 72, 256), F32),
             pltpu.SemaphoreType.DMA((len(COPIES),)),
             pltpu.SemaphoreType.DMA((len(COPIES),)),
             pltpu.SemaphoreType.DMA((4,)),

time: 60.3 us -> 57.3 us (0.950)
  Pallas kernels: 56.7 us -> 54 us
    pallas_call x1, Pallas kernels: 56.7 us -> 54 us  [on_device(): pl.pallas_call(kernel, out_shape=jax.ShapeDtypeStruct((ROWS, 1024), F32),...]
where the time goes in v2:
time: 57.3 us; the launch traced here: 57.1 us
  Pallas kernels  54 us (94%)
  local copies, waits for them, and re-layouts  3.16 us (6%)
    pallas_call x1, Pallas kernels, on_device(): pl.pallas_call(kernel, out_shape=jax.ShapeDtypeStruct((ROWS, 1024), F32),...  54 us
    unnamed x1, local copies, waits for them, and re-layouts  3.16 us

profile of v2, /device:TPU:40, one launch (start us, length us, event | category | flops | bytes accessed | tf_op | source)
XLA Modules:
  0.0 57.1 jit_solution(10198122226257384915)
XLA Ops:
  0.0 54.0 %shard_map.46 = f32[512,1024]{1,0:T(8,128)} custom-call(bf16[2048,1024]{1,0:T(8,128)(2,1)} %tokens_hbm.1, f32[1,1024]{1,0:T(1,128)} %bitcast.3, bf16[3,1024,256]{2,1,0:T(8,128)(2,1)} %bitcast.2, bf16[256,1024]{1,0:T(8,128)(2,1)} %wout_hbm.1), custom_call_target="tpu_custom_call" | custom-call | tf_op jit(solution)/shard_map/pallas_call | solution.py:451
  54.0 3.2 %copy.6 = f32[512,1024]{1,0:T(8,128)} copy(f32[512,1024]{1,0:T(8,128)} %shard_map.46) | data formatting | bytes 4194304

commit v3 on v2

--- a/solution.py
+++ b/solution.py
@@ -45,7 +45,7 @@
     tokens_hbm, gain_ref, wqkv_hbm, wout_hbm, out_ref,
     tok, wq, normed, pp, kd, qt, vt, kvm, qm, qmp, vtm, kvff, kvf, qff, qf, qfp, vtf,
     pm_own, pm_st, pm_r, pf_st, pf_r, locacc, att_st, att_r, fx_st, fx_r, wo, s0, s1, s2, mid_all,
-    send_sem, recv_sem, tok_sem, w_sem, wo_sem,
+    send_sem, recv_sem, tok_sem, w_sem, wo_sem, total, out_sem,
 ):
     seq = lax.axis_index("seq")
     g = lax.axis_index("head")
@@ -429,7 +429,11 @@
             for t in range(2):
                 pp[0, t, pl.ds(8 * (m % 8) + m // 8, 8, stride=64), :] = turned[8 * m:8 * m + 8, 128 * t:128 * t + 128]
         rows = jnp.concatenate([pp[0, 0], pp[0, 1]], axis=1).astype(BF16)
-        return dot(rows, wo[k]).astype(BF16).astype(F32)
+        return rows
+
+    def out_copy(q):
+        here = pl.ds(q * 128, 128)
+        return pltpu.make_async_copy(total.at[here], out_ref.at[here], out_sem.at[q])
 
     for n, k in enumerate((3, 2, 0, 1)):
         if k < 3:
@@ -438,10 +442,18 @@
             arrived("w2")
         if k == 2:
             arrived("wc")
-        if n == 0:
-            out_ref[...] = contribution(k)
-        else:
-            out_ref[...] += contribution(k)
+        turned = contribution(k)
+        for q in range(4):
+            here = pl.ds(q * 128, 128)
+            product = dot(turned[q * 128:(q + 1) * 128], wo[k]).astype(BF16).astype(F32)
+            if n == 0:
+                total[here, :] = product
+            else:
+                total[here, :] += product
+            if n == 3:
+                out_copy(q).start()
+    for q in range(4):
+        out_copy(q).wait()
     for name in COPIES:
         copy(name).wait_send()
 
@@ -457,7 +469,7 @@
             pl.BlockSpec(memory_space=pl.ANY),
             pl.BlockSpec(memory_space=pl.ANY),
         ],
-        out_specs=pl.BlockSpec(memory_space=pltpu.VMEM),
+        out_specs=pl.BlockSpec(memory_space=pl.ANY),
         scratch_shapes=[
             vm((4, ROWS, 1024), BF16),
             vm((3, 1024, FEATS), BF16),
@@ -496,6 +508,8 @@
             pltpu.SemaphoreType.DMA((4,)),
             pltpu.SemaphoreType.DMA((3,)),
             pltpu.SemaphoreType.DMA,
+            vm((ROWS, 1024), F32),
+            pltpu.SemaphoreType.DMA((4,)),
         ],
         compiler_params=pltpu.CompilerParams(
             collective_id=0, has_side_effects=True, vmem_limit_bytes=56 * 1024 * 1024

time: 57.3 us -> 57.1 us (level)
  no operation moved by 1% of the time
where the time goes in v3:
time: 57.1 us; the launch traced here: 57 us
  Pallas kernels  53.8 us (94%)
  local copies, waits for them, and re-layouts  3.16 us (6%)
    pallas_call x1, Pallas kernels, on_device(): pl.pallas_call(kernel, out_shape=jax.ShapeDtypeStruct((ROWS, 1024), F32),...  53.8 us
    unnamed x1, local copies, waits for them, and re-layouts  3.16 us

profile of v3, /device:TPU:40, one launch (start us, length us, event | category | flops | bytes accessed | tf_op | source)
XLA Modules:
  0.0 57.0 jit_solution(11684678997689130948)
XLA Ops:
  0.0 53.8 %shard_map.46 = f32[512,1024]{1,0:T(8,128)} custom-call(bf16[2048,1024]{1,0:T(8,128)(2,1)} %tokens_hbm.1, f32[1,1024]{1,0:T(1,128)} %bitcast.3, bf16[3,1024,256]{2,1,0:T(8,128)(2,1)} %bitcast.2, bf16[256,1024]{1,0:T(8,128)(2,1)} %wout_hbm.1), custom_call_target="tpu_custom_call" | custom-call | tf_op jit(solution)/shard_map/pallas_call | solution.py:463
  53.8 3.2 %copy.6 = f32[512,1024]{1,0:T(8,128)} copy(f32[512,1024]{1,0:T(8,128)} %shard_map.46) | data formatting | bytes 4194304
